TPU v7x, 256 devices: a whole 4x4x8 slice. The times are simulated.
256 devices in a mesh: ctx: 32 (over y, z), ch: 8 (over x, core).
Axes of the slice: x: 4, y: 4, z: 8, core: 2. Of those that a mesh axis runs over, the one named last changes fastest.
Arguments:
- gate_in: bfloat16 [512, 131072], P('ch', 'ctx'), may hold values from -64 to 64
- key_in: bfloat16 [512, 131072], P('ch', 'ctx'), may hold values from -6 to 6
- value_in: bfloat16 [512, 131072], P('ch', 'ctx'), may hold values from -6 to 6
- long_filter: float32 [512, 131072], P('ch', 'ctx'), may hold values from -0.015625 to 0.015625
- skip_weight: float32 [512], P('ch'), may hold values from -1 to 1
- norm_gain: float32 [512], P('ch'), may hold values from 0.1 to 1.9
Outputs:
- mixed: bfloat16 [512, 131072], P('ch', 'ctx')
All inputs are finite; a program needn't handle non-finite values.
Results may differ from a plain program's by a relative error of at most 0.001.
Values sent between devices are 32-bit elements; how exact they have to be, the bound alone decides.
A program may use at most 128 MiB of HBM per device.

v0:
```python
import math

import jax
import jax.numpy as jnp
from jax import lax
from jax.sharding import PartitionSpec as P

FACTOR = 32


HIGH = lax.Precision.HIGHEST


def shifted(block, axis, distance):
    devices = range(lax.axis_size(axis))
    route = [(i - distance, i) for i in devices if i - distance in devices]
    return lax.ppermute(block, axis, route)


def angle_table(count_a, count_b, period):
    prod = (
        jnp.arange(count_a, dtype=jnp.int32)[:, None]
        * jnp.arange(count_b, dtype=jnp.int32)[None, :]
        % period
    )
    angle = 2.0 * math.pi / period * prod.astype(jnp.float32)
    return (jnp.cos(angle), jnp.sin(angle))


def forward_spectrum(signal, factor):
    rows, half = signal.shape
    length = 2 * half
    width = length // factor
    folded = signal.reshape(rows, factor // 2, width)
    cos_one, sin_one = angle_table(factor, factor // 2, factor)
    real_one = jnp.einsum("kn,cns->cks", cos_one, folded, precision=HIGH)
    imag_one = -jnp.einsum("kn,cns->cks", sin_one, folded, precision=HIGH)
    tw_cos, tw_sin = angle_table(factor, width, length)
    real_two = real_one * tw_cos + imag_one * tw_sin
    imag_two = imag_one * tw_cos - real_one * tw_sin
    cos_two, sin_two = angle_table(width, width, width)
    real_out = jnp.matmul(real_two, cos_two, precision=HIGH) + jnp.matmul(
        imag_two, sin_two, precision=HIGH
    )
    imag_out = jnp.matmul(imag_two, cos_two, precision=HIGH) - jnp.matmul(
        real_two, sin_two, precision=HIGH
    )
    return jnp.stack([real_out, imag_out])


def inverse_signal(spectrum, factor, keep):
    real_in, imag_in = (spectrum[0], spectrum[1])
    rows = real_in.shape[0]
    width = real_in.shape[2]
    length = factor * width
    cos_two, sin_two = angle_table(width, width, width)
    real_a = jnp.matmul(real_in, cos_two, precision=HIGH) - jnp.matmul(
        imag_in, sin_two, precision=HIGH
    )
    imag_a = jnp.matmul(imag_in, cos_two, precision=HIGH) + jnp.matmul(
        real_in, sin_two, precision=HIGH
    )
    tw_cos, tw_sin = angle_table(factor, width, length)
    real_b = real_a * tw_cos - imag_a * tw_sin
    imag_b = imag_a * tw_cos + real_a * tw_sin
    cos_one, sin_one = angle_table(keep, factor, factor)
    out = jnp.einsum("nk,cks->cns", cos_one, real_b, precision=HIGH) - jnp.einsum(
        "nk,cks->cns", sin_one, imag_b, precision=HIGH
    )
    return (out / length).reshape(rows, keep * width)


def block_forward(spectrum, blocks):
    cos_w, sin_w = angle_table(2 * blocks, blocks, 2 * blocks)
    real_part = jnp.einsum("pe,cejs->cpjs", cos_w, spectrum[0], precision=HIGH) + jnp.einsum(
        "pe,cejs->cpjs", sin_w, spectrum[1], precision=HIGH
    )
    imag_part = jnp.einsum("pe,cejs->cpjs", cos_w, spectrum[1], precision=HIGH) - jnp.einsum(
        "pe,cejs->cpjs", sin_w, spectrum[0], precision=HIGH
    )
    return (real_part, imag_part)


def convolve_blocks(driven_spec, filter_spec, blocks):
    real_u, imag_u = block_forward(driven_spec, blocks)
    real_h, imag_h = block_forward(filter_spec, blocks)
    real_p = real_u * real_h - imag_u * imag_h
    imag_p = real_u * imag_h + imag_u * real_h
    cos_w, sin_w = angle_table(blocks, 2 * blocks, 2 * blocks)
    scale = 1.0 / (2 * blocks)
    real_z = (
        jnp.einsum("ep,cpjs->cejs", cos_w, real_p, precision=HIGH)
        - jnp.einsum("ep,cpjs->cejs", sin_w, imag_p, precision=HIGH)
    ) * scale
    imag_z = (
        jnp.einsum("ep,cpjs->cejs", cos_w, imag_p, precision=HIGH)
        + jnp.einsum("ep,cpjs->cejs", sin_w, real_p, precision=HIGH)
    ) * scale
    return jnp.stack([real_z, imag_z])


def body(gate_in, key_in, value_in, long_filter, skip_weight, norm_gain):
    channels, block_len = gate_in.shape
    driven = key_in.astype(jnp.float32) * value_in.astype(jnp.float32)
    blocks = lax.axis_size("ctx")
    driven_spec = forward_spectrum(driven, FACTOR)[:, :, None]
    filter_spec = forward_spectrum(long_filter, FACTOR)[:, :, None]
    driven_blocks, filter_blocks = (
        lax.all_to_all(driven_spec, "ctx", split_axis=3, concat_axis=2, tiled=True),
        lax.all_to_all(filter_spec, "ctx", split_axis=3, concat_axis=2, tiled=True),
    )
    product = convolve_blocks(driven_blocks, filter_blocks, blocks)
    returned = lax.all_to_all(product, "ctx", split_axis=2, concat_axis=3, tiled=True)[:, :, 0]
    whole = inverse_signal(returned, FACTOR, FACTOR)
    result = whole[:, :block_len] + shifted(whole[:, block_len:], "ctx", 1)
    branch = gate_in.astype(jnp.float32) * (result + skip_weight[:, None] * driven)
    total = lax.psum(jnp.sum(branch * branch, axis=0), "ch")
    power = total / (channels * lax.axis_size("ch"))
    mixed = branch * norm_gain[:, None] * lax.rsqrt(power + 1e-06)[None, :]
    return mixed.astype(jnp.bfloat16)


def solution(mesh):
    in_specs = (P("ch", "ctx"), P("ch", "ctx"), P("ch", "ctx"), P("ch", "ctx"), P("ch"), P("ch"))
    out_specs = P("ch", "ctx")
    return jax.shard_map(body, mesh=mesh, in_specs=in_specs, out_specs=out_specs, check_vma=False)
```

profile of v0, /device:TPU:32, one launch (start us, length us, event | category | flops | bytes accessed | tf_op | source)
XLA Modules:
  0.0 453.0 jit_solution(1834577108372435936)
XLA Ops:
  0.0 1.5 copy.23
  1.5 1.9 fusion.139
  3.4 1.9 fusion.135
  5.5 3.0 fusion.8
  8.5 3.0 fusion.10
  11.5 3.4 subtract_bitcast_fusion
  14.9 3.0 add_bitcast_fusion
  17.9 0.6 maximum_bitcast_fusion.1
  18.5 4.4 copy.10
  22.9 11.7 %all-to-all-start.1 = ((f32[2,64,1,32,256]{4,1,0,2,3:T(8,128)}), f32[2,64,1,32,256]{4,1,0,2,3:T(8,128)}, u32[]{:S(2)}, u32[]{:S(2)}) async-start(f32[2,64,1,32,256]{4,1,0,2,3:T(8,128)} %copy.10), calls=%async_computation.1 | async-start | bytes 8388608 | tf_op jit(solution)/shard_map/all_to_all | solution.py:110
  35.1 1.9 fusion.141
  37.0 1.9 fusion.137
  38.9 3.0 fusion.52
  41.9 3.0 subtract_bitcast_fusion.1
  44.8 3.2 fusion.56
  48.0 2.9 add_bitcast_fusion.1
  51.0 0.6 maximum_bitcast_fusion
  51.6 4.4 copy.7
  56.0 74.0 %all-to-all-done.1 = f32[2,64,1,32,256]{4,1,0,2,3:T(8,128)} async-done(((f32[2,64,1,32,256]{4,1,0,2,3:T(8,128)}), f32[2,64,1,32,256]{4,1,0,2,3:T(8,128)}, u32[]{:S(2)}, u32[]{:S(2)}) %all-to-all-start.1) | async-done | bytes 4194336 | tf_op jit(solution)/shard_map/all_to_all | solution.py:110
  130.0 7.3 %all-to-all-start = ((f32[2,64,1,32,256]{4,1,0,2,3:T(8,128)}), f32[2,64,1,32,256]{4,1,0,2,3:T(8,128)}, u32[]{:S(2)}, u32[]{:S(2)}) async-start(f32[2,64,1,32,256]{4,1,0,2,3:T(8,128)} %copy.7), calls=%async_computation | async-start | bytes 8388608 | tf_op jit(solution)/shard_map/all_to_all | solution.py:109
  137.3 2.5 fusion.292
  139.8 5.0 %fusion.28 = f32[64,256,64]{1,2,0:T(8,128)S(1)} fusion(f32[1,64,1,32,256]{4,1,0,2,3:T(8,128)S(1)} %get-tuple-element.11), kind=kOutput, calls=%fused_computation.56 | convolution fusion | flops 402681856 | bytes 6291456 | tf_op jit(solution)/shard_map/pe,cejs->cpjs/dot_general | solution.py:75
  144.8 5.9 %fusion.29 = f32[64,256,64]{1,2,0:T(8,128)} fusion(f32[1,64,1,32,256]{4,1,0,2,3:T(8,128)S(1)} %get-tuple-element.12), kind=kOutput, calls=%fused_computation.57 | convolution fusion | flops 402681856 | bytes 6291456 | tf_op jit(solution)/shard_map/pe,cejs->cpjs/dot_general | solution.py:78
  150.8 6.2 %convolution_add_fusion = f32[64,256,64]{1,2,0:T(8,128)} fusion(f32[64,256,64]{1,2,0:T(8,128)S(1)} %fusion.28, f32[1,64,1,32,256]{4,1,0,2,3:T(8,128)S(1)} %get-tuple-element.12), kind=kOutput, calls=%fused_computation.15 | convolution fusion | flops 403730432 | bytes 10485760 | tf_op jit(solution)/shard_map/pe,cejs->cpjs/dot_general | solution.py:75
  157.0 75.2 %all-to-all-done = f32[2,64,1,32,256]{4,1,0,2,3:T(8,128)} async-done(((f32[2,64,1,32,256]{4,1,0,2,3:T(8,128)}), f32[2,64,1,32,256]{4,1,0,2,3:T(8,128)}, u32[]{:S(2)}, u32[]{:S(2)}) %all-to-all-start) | async-done | bytes 4194336 | tf_op jit(solution)/shard_map/all_to_all | solution.py:109
  232.2 2.6 fusion.293
  234.8 4.9 %fusion.26 = f32[64,256,64]{1,2,0:T(8,128)S(1)} fusion(f32[1,64,1,32,256]{4,1,0,2,3:T(8,128)S(1)} %get-tuple-element.13), kind=kOutput, calls=%fused_computation.54 | convolution fusion | flops 402681856 | bytes 6291456 | tf_op jit(solution)/shard_map/pe,cejs->cpjs/dot_general | solution.py:75
  239.7 4.9 %fusion.27 = f32[64,256,64]{1,2,0:T(8,128)S(1)} fusion(f32[1,64,1,32,256]{4,1,0,2,3:T(8,128)S(1)} %get-tuple-element.14), kind=kOutput, calls=%fused_computation.55 | convolution fusion | flops 402681856 | bytes 6291456 | tf_op jit(solution)/shard_map/pe,cejs->cpjs/dot_general | solution.py:78
  244.6 5.1 %convolution_add_fusion.1 = f32[64,256,64]{1,2,0:T(8,128)S(1)} fusion(f32[64,256,64]{1,2,0:T(8,128)S(1)} %fusion.26, f32[1,64,1,32,256]{4,1,0,2,3:T(8,128)S(1)} %get-tuple-element.14), kind=kOutput, calls=%fused_computation.16 | convolution fusion | flops 403730432 | bytes 10485760 | tf_op jit(solution)/shard_map/pe,cejs->cpjs/dot_general | solution.py:75
  249.7 6.1 %convolution_subtract_fusion = f32[64,256,64]{1,2,0:T(8,128)} fusion(f32[64,256,64]{1,2,0:T(8,128)S(1)} %copy-done, f32[1,64,1,32,256]{4,1,0,2,3:T(8,128)S(1)} %get-tuple-element.11), kind=kOutput, calls=%fused_computation.13 | convolution fusion | flops 403730432 | bytes 10485760 | tf_op jit(solution)/shard_map/pe,cejs->cpjs/dot_general | solution.py:78
  255.9 8.0 %multiply_add_fusion = (f32[64,256,64]{1,2,0:T(8,128)S(1)}, f32[64,256,64]{1,2,0:T(8,128)S(1)}) fusion(f32[64,256,64]{1,2,0:T(8,128)S(1)} %copy-done.1, f32[64,256,64]{1,2,0:T(8,128)S(1)} %convolution_add_fusion.1, f32[64,256,64]{1,2,0:T(8,128)} %convolution_subtract_fusion, f32[64,256,64]{1,2,0:T(8,128)S(1)} %fusion.27, ...), kind=kOutput, calls=%fused_computation.11 | convolution fusion | flops 410021888 | bytes 27262976 | tf_op jit(solution)/shard_map/pe,cejs->cpjs/dot_general | solution.py:78
  263.9 2.7 fusion
  266.5 2.6 fusion.2
  269.2 2.8 multiply_bitcast_fusion
  272.0 2.8 multiply_bitcast_fusion.1
  275.4 2.6 copy.13
  278.0 102.7 %all_to_all.12 = f32[2,64,32,1,256]{4,1,3,0,2:T(8,128)S(1)} all-to-all(f32[2,64,32,1,256]{4,1,3,0,2:T(8,128)S(1)} %copy.13), channel_id=1, replica_groups=mesh['ctx'=32,'ch'=8] {'ctx'}, dimensions={2} | all-to-all | bytes 8388608 | tf_op jit(solution)/shard_map/all_to_all | solution.py:113
  381.1 3.9 fusion.31
  385.0 3.9 fusion.30
  388.9 4.1 fusion.38
  393.1 3.9 fusion.39
  397.0 2.2 fusion.18
  399.2 2.3 subtract_multiply_fusion
  401.6 1.2 copy.24
  402.9 2.1 collective-permute-start
  404.9 22.7 %collective-permute-done = f32[64,4096]{1,0:T(8,128)S(1)} collective-permute-done((f32[64,4096]{1,0:T(8,128)S(1)}, f32[64,4096]{1,0:T(8,128)S(1)}, u32[]{:S(2)}, u32[]{:S(2)}) %collective-permute-start) | collective-permute-done | bytes 1048608 | tf_op jit(solution)/shard_map/ppermute | solution.py:17
  428.1 23.6 %psum.7 = f32[4096]{0:T(1024)S(1)} all-reduce(f32[4096]{0:T(1024)S(1)} %get-tuple-element.5), channel_id=1, replica_groups=mesh['ctx'=32,'ch'=8] {'ch'}, use_global_device_ids=true, to_apply=%region_1.2 | all-reduce | flops 4096 | bytes 32768 | tf_op jit(solution)/shard_map/psum | solution.py:117
  451.7 1.0 multiply_convert_fusion
  (22 shorter events, 2.2 us)
Async XLA Ops:
  22.9 11.7 %copy-start.2 = (bf16[64,4096]{1,0:T(8,128)(2,1)S(1)}, bf16[64,4096]{1,0:T(8,128)(2,1)}, u32[]{:S(2)}) copy-start(bf16[64,4096]{1,0:T(8,128)(2,1)} %param.8) | copy-start | bytes 1572868
  22.9 11.7 %copy-start.3 = (bf16[64,4096]{1,0:T(8,128)(2,1)S(1)}, bf16[64,4096]{1,0:T(8,128)(2,1)}, u32[]{:S(2)}) copy-start(bf16[64,4096]{1,0:T(8,128)(2,1)} %param.7) | copy-start | bytes 1572868
  22.9 107.1 %all-to-all-start.1 = ((f32[2,64,1,32,256]{4,1,0,2,3:T(8,128)}), f32[2,64,1,32,256]{4,1,0,2,3:T(8,128)}, u32[]{:S(2)}, u32[]{:S(2)}) async-start(f32[2,64,1,32,256]{4,1,0,2,3:T(8,128)} %copy.10), calls=%async_computation.1 | async-start | bytes 8388608 | tf_op jit(solution)/shard_map/all_to_all | solution.py:110
  130.0 102.2 %all-to-all-start = ((f32[2,64,1,32,256]{4,1,0,2,3:T(8,128)}), f32[2,64,1,32,256]{4,1,0,2,3:T(8,128)}, u32[]{:S(2)}, u32[]{:S(2)}) async-start(f32[2,64,1,32,256]{4,1,0,2,3:T(8,128)} %copy.7), calls=%async_computation | async-start | bytes 8388608 | tf_op jit(solution)/shard_map/all_to_all | solution.py:109
  244.6 5.1 %copy-start = (f32[64,256,64]{1,2,0:T(8,128)S(1)}, f32[64,256,64]{1,2,0:T(8,128)}, u32[]{:S(2)}) copy-start(f32[64,256,64]{1,2,0:T(8,128)} %fusion.29) | copy-start | bytes 12582916
  249.7 6.2 %copy-start.1 = (f32[64,256,64]{1,2,0:T(8,128)S(1)}, f32[64,256,64]{1,2,0:T(8,128)}, u32[]{:S(2)}) copy-start(f32[64,256,64]{1,2,0:T(8,128)} %convolution_add_fusion) | copy-start | bytes 12582916
  402.8 24.9 %copy-start.4 = (bf16[64,4096]{1,0:T(8,128)(2,1)S(1)}, bf16[64,4096]{1,0:T(8,128)(2,1)}, u32[]{:S(2)}) copy-start(bf16[64,4096]{1,0:T(8,128)(2,1)} %param.6) | copy-start | bytes 1572868
  402.8 24.9 %copy-start.5 = (f32[64]{0:T(128)S(1)}, f32[64]{0:T(128)}, u32[]{:S(2)}) copy-start(f32[64]{0:T(128)} %param.10) | copy-start | bytes 772
  402.9 48.8 %copy-start.6 = (f32[64]{0:T(128)S(1)}, f32[64]{0:T(128)}, u32[]{:S(2)}) copy-start(f32[64]{0:T(128)} %param.11) | copy-start | bytes 772
  402.9 24.8 %collective-permute-start = (f32[64,4096]{1,0:T(8,128)S(1)}, f32[64,4096]{1,0:T(8,128)S(1)}, u32[]{:S(2)}, u32[]{:S(2)}) collective-permute-start(f32[64,4096]{1,0:T(8,128)S(1)} %slice.52), channel_id=1, source_target_pairs={{0,8},{8,16},{16,24},{24,32},{32,40},{40,48},{48,56},{56,64},{64,7... | collective-permute-start | bytes 3145736 | tf_op jit(solution)/shard_map/ppermute | solution.py:17
where the time goes:
time: 462 us; the launch traced here: 453 us
  waiting for transfers between devices  172 us (37%)
  blocking collectives  126 us (27%)
  matrix products  109 us (24%)
  starting transfers between devices  21.1 us (5%)
  local copies, waits for them, and re-layouts  20.2 us (4%)
    all_to_all x1, blocking collectives, body(): lax.all_to_all(product, 'ctx', split_axis=2, concat_axis=3, tiled=True)  103 us
    all_to_all x1, waiting for transfers between devices, body(): lax.all_to_all(driven_spec, 'ctx', split_axis=3, concat_axis=2, tiled=True)  75.2 us
    all_to_all x1, waiting for transfers between devices, body(): lax.all_to_all(filter_spec, 'ctx', split_axis=3, concat_axis=2, tiled=True)  74 us
    psum x1, blocking collectives, body(): total = lax.psum(jnp.sum(branch * branch, axis=0), 'ch')  23.6 us
    ppermute x1, waiting for transfers between devices, shifted(): return lax.ppermute(block, axis, route)  22.7 us
    dot_general x2, matrix products, block_forward(): jnp.einsum('pe,cejs->cpjs', sin_w, spectrum[0], precision=HIGH)  14.1 us
    all_to_all x1, starting transfers between devices, body(): lax.all_to_all(filter_spec, 'ctx', split_axis=3, concat_axis=2, tiled=True)  11.7 us
    dot_general x2, matrix products, block_forward(): jnp.einsum('pe,cejs->cpjs', sin_w, spectrum[1], precision=HIGH)  11.4 us
  transfers between devices with their start and end apart: 3, of which 3 were waited for; matrix products, arithmetic and copies ran while one was open for 9% of the time, Pallas kernels for 0%

commit v1 on v0

v1 whole, which is shorter than its diff:
```python
import jax
import jax.numpy as jnp
import numpy as np
from jax import lax
from jax.sharding import PartitionSpec as P

ROWS = 512
COLS = 256
SIZE = ROWS * COLS
SLOTS = 2
HIGH = lax.Precision.HIGH


def turn(num, den):
    angle = 2.0 * np.pi * ((num % den) / den)
    return np.cos(angle).astype(np.float32), (-np.sin(angle)).astype(np.float32)


def tables():
    freq = 4 * np.arange(ROWS, dtype=np.int64) + 1
    rows = np.arange(ROWS, dtype=np.int64)
    cols = np.arange(COLS, dtype=np.int64)
    first = turn(freq[:, None] * rows[None, :], 4 * ROWS)
    twiddle = turn(freq[:, None] * cols[None, :], 4 * SIZE)
    second = turn(cols[:, None] * cols[None, :], COLS)
    return first, twiddle, second


def body(gate_in, key_in, value_in, long_filter, skip_weight, norm_gain):
    channels, block = gate_in.shape
    blocks = lax.axis_size("ctx")
    (f_re, f_im), (t_re, t_im), (s_re, s_im) = tables()
    driven = key_in.astype(jnp.float32) * value_in.astype(jnp.float32)
    both = jnp.stack([driven, long_filter]).reshape(2, SLOTS, blocks, block // COLS, COLS)
    both = lax.all_to_all(both, "ctx", split_axis=2, concat_axis=2, tiled=True)
    both = both.reshape(2 * SLOTS, ROWS, COLS)
    first = np.concatenate([f_re, f_im])
    a = jnp.einsum("kr,brl->bkl", first, both, precision=HIGH)
    a_re, a_im = a[:, :ROWS], a[:, ROWS:]
    b = jnp.concatenate([a_re * t_re - a_im * t_im, a_re * t_im + a_im * t_re], axis=-1)
    second = np.block([[s_re, s_im], [-s_im, s_re]])
    spec = jnp.einsum("bkl,lm->bkm", b, second, precision=HIGH)
    x_re, x_im = spec[:SLOTS, :, :COLS], spec[:SLOTS, :, COLS:]
    h_re, h_im = spec[SLOTS:, :, :COLS], spec[SLOTS:, :, COLS:]
    prod = jnp.concatenate([x_re * h_re - x_im * h_im, x_re * h_im + x_im * h_re], axis=-1)
    back = np.block([[s_re, -s_im], [s_im, s_re]]) / np.float32(SIZE)
    c = jnp.einsum("bkm,ml->bkl", prod, back, precision=HIGH)
    c_re, c_im = c[..., :COLS], c[..., COLS:]
    d = jnp.concatenate([c_re * t_re + c_im * t_im, c_im * t_re - c_re * t_im], axis=1)
    last = np.concatenate([f_re, f_im]).T
    conv = jnp.einsum("rk,bkl->brl", last, d, precision=HIGH)
    conv = conv.reshape(SLOTS, blocks, block // COLS, COLS)
    conv = lax.all_to_all(conv, "ctx", split_axis=1, concat_axis=1, tiled=True)
    conv = conv.reshape(channels, block)
    branch = gate_in.astype(jnp.float32) * (conv + skip_weight[:, None] * driven)
    total = lax.psum(jnp.sum(branch * branch, axis=0), "ch")
    power = total / (channels * lax.axis_size("ch"))
    mixed = branch * norm_gain[:, None] * lax.rsqrt(power + 1e-6)[None, :]
    return mixed.astype(jnp.bfloat16)


def solution(mesh):
    specs = (P("ch", "ctx"), P("ch", "ctx"), P("ch", "ctx"), P("ch", "ctx"), P("ch"), P("ch"))
    return jax.shard_map(body, mesh=mesh, in_specs=specs, out_specs=P("ch", "ctx"), check_vma=False)
```

time: 462 us -> 147 us (0.32)
  the two profiles are of different devices: /device:TPU:32 before, /device:TPU:1 now
where the time goes in v1:
time: 147 us; the launch traced here: 145 us
  blocking collectives  117 us (80%)
  matrix products  16.8 us (11%)
  local copies, waits for them, and re-layouts  7.63 us (5%)
  other arithmetic  3.41 us (2%)
    all_to_all x1, blocking collectives, body(): both = lax.all_to_all(both, 'ctx', split_axis=2, concat_axis=2, tiled=True)  58.9 us
    all_to_all x1, blocking collectives, body(): conv = lax.all_to_all(conv, 'ctx', split_axis=1, concat_axis=1, tiled=True)  33.2 us
    psum x1, blocking collectives, body(): total = lax.psum(jnp.sum(branch * branch, axis=0), 'ch')  25 us
    dot_general x1, matrix products, body(): a = jnp.einsum('kr,brl->bkl', first, both, precision=HIGH)  7.03 us
    unnamed x29, local copies, waits for them, and re-layouts  6.72 us
    dot_general x1, matrix products, body(): spec = jnp.einsum('bkl,lm->bkm', b, second, precision=HIGH)  4.18 us
    dot_general x1, matrix products, body(): conv = jnp.einsum('rk,bkl->brl', last, d, precision=HIGH)  3.54 us

profile of v1, /device:TPU:1, one launch (start us, length us, event | category | flops | bytes accessed | tf_op | source)
XLA Modules:
  0.0 145.2 jit_solution(6021192654936331747)
XLA Ops:
  0.0 0.0 copy-start
  0.0 0.0 copy-start.1
  0.0 1.6 %copy.53 = f32[8,8,16,256]{3,2,1,0:T(8,128)S(1)} copy(f32[8,8,16,256]{3,1,2,0:T(8,128)} %bitcast.32) | data formatting | bytes 2097152
  1.6 0.0 copy-done
  1.6 0.0 copy-done.1
  1.7 0.1 convert_multiply_fusion
  1.8 0.3 copy.52
  2.1 0.2 pad_maximum_fusion
  2.3 0.2 copy.37
  2.5 58.9 %all_to_all.10 = f32[2,2,32,16,256]{4,3,1,0,2:T(8,128)S(1)} all-to-all(f32[2,2,32,16,256]{4,3,1,0,2:T(8,128)S(1)} %copy.37), channel_id=1, replica_groups=mesh['ctx'=32,'ch'=8] {'ctx'}, dimensions={2} | all-to-all | bytes 4194304 | tf_op jit(solution)/shard_map/all_to_all | solution.py:35
  61.5 0.0 copy-start.3
  61.5 0.2 copy.38
  61.6 1.4 copy-done.3
  63.0 0.0 copy-start.9
  63.0 0.0 copy-start.10
  63.1 7.0 %convolution_bitcast_fusion = f32[4,1024,256]{1,2,0:T(8,128)S(1)} fusion(f32[4,512,256]{2,1,0:T(8,128)S(1)} %bitcast.26, f32[1024,512,1]{1,0,2:T(8,128)S(1)} %copy-done.3), kind=kOutput, calls=%fused_computation.4 | convolution fusion | flops 3221225472 | bytes 8388608 | tf_op jit(solution)/shard_map/kr,brl->bkl/dot_general | solution.py:38
  70.1 0.0 copy-done.9
  70.1 0.0 copy-done.10
  70.1 0.0 copy-start.6
  70.1 0.9 multiply_subtract_fusion
  71.0 0.3 copy-done.6
  71.3 4.2 %fusion = f32[4,512,512]{1,2,0:T(8,128)S(1)} fusion(f32[512,512,1]{0,1,2:T(8,128)S(1)} %copy-done.6, f32[4,512,256]{1,2,0:T(8,128)S(1)} %get-tuple-element.6, f32[4,512,256]{1,2,0:T(8,128)S(1)} %get-tuple-element.5), kind=kOutput, calls=%fused_computation | convolution fusion | flops 3222274048 | bytes 9437184 | tf_op jit(solution)/shard_map/bkl,lm->bkm/dot_general | solution.py:42
  75.5 0.0 copy-start.5
  75.5 0.5 multiply_subtract_fusion.2
  76.1 0.7 copy-done.5
  76.8 0.0 copy-start.7
  76.8 0.0 copy-start.8
  76.8 2.1 %fusion.4 = f32[2,512,512]{2,1,0:T(8,128)S(1)} fusion(f32[512,512,1]{1,0,2:T(8,128)S(1)} %copy-done.5, f32[2,512,256]{1,2,0:T(8,128)S(1)} %get-tuple-element.8, f32[2,512,256]{1,2,0:T(8,128)S(1)} %get-tuple-element.7), kind=kOutput, calls=%fused_computation.6 | convolution fusion | flops 1611137024 | bytes 5242880 | tf_op jit(solution)/shard_map/bkm,ml->bkl/dot_general | solution.py:47
  78.8 0.0 copy-done.7
  78.8 0.0 copy-done.8
  78.9 0.0 copy-start.2
  78.9 0.2 multiply_add_fusion.1
  79.1 1.3 copy-done.2
  80.4 3.5 %fusion.12 = f32[2,512,256]{1,2,0:T(8,128)S(1)} fusion(f32[512,1024,1]{1,0,2:T(8,128)S(1)} %copy-done.2, f32[2,512,256]{2,1,0:T(8,128)S(1)} %get-tuple-element.10, f32[2,512,256]{2,1,0:T(8,128)S(1)} %get-tuple-element.9), kind=kOutput, calls=%fused_computation.16 | convolution fusion | flops 1611137024 | bytes 5242880 | tf_op jit(solution)/shard_map/rk,bkl->brl/dot_general | solution.py:51
  84.0 0.3 copy.45
  84.3 0.1 copy.46
  84.4 33.2 %all_to_all.11 = f32[2,32,16,256]{3,2,0,1:T(8,128)S(1)} all-to-all(f32[2,32,16,256]{3,2,0,1:T(8,128)S(1)} %copy.46), channel_id=1, replica_groups=mesh['ctx'=32,'ch'=8] {'ctx'}, dimensions={1} | all-to-all | bytes 2097152 | tf_op jit(solution)/shard_map/all_to_all | solution.py:53
  117.6 0.0 copy-start.4
  117.6 0.0 copy-start.11
  117.6 0.1 copy.47
  117.7 0.0 copy-start.12
  117.7 0.6 copy.54
  118.3 0.3 copy-done.4
  118.6 0.0 copy-done.11
  118.6 0.4 multiply_reduce_fusion
  119.0 25.0 %psum.7 = f32[4096]{0:T(1024)S(1)} all-reduce(f32[4096]{0:T(1024)S(1)} %multiply_reduce_fusion), channel_id=1, replica_groups=mesh['ctx'=32,'ch'=8] {'ch'}, use_global_device_ids=true, to_apply=%region_1.0 | all-reduce | flops 4096 | bytes 32768 | tf_op jit(solution)/shard_map/psum | solution.py:56
  144.0 0.0 copy-done.12
  144.0 1.2 multiply_convert_fusion
  (1 shorter events, 0.0 us)
Async XLA Ops:
  0.0 1.6 %copy-start = (bf16[64,4096]{1,0:T(8,128)(2,1)S(1)}, bf16[64,4096]{1,0:T(8,128)(2,1)}, u32[]{:S(2)}) copy-start(bf16[64,4096]{1,0:T(8,128)(2,1)} %param.14) | copy-start | bytes 1572868
  0.0 1.6 %copy-start.1 = (bf16[64,4096]{1,0:T(8,128)(2,1)S(1)}, bf16[64,4096]{1,0:T(8,128)(2,1)}, u32[]{:S(2)}) copy-start(bf16[64,4096]{1,0:T(8,128)(2,1)} %param.13) | copy-start | bytes 1572868
  61.5 1.6 %copy-start.3 = (f32[1024,512,1]{1,0,2:T(8,128)S(1)}, f32[1024,512,1]{1,0,2:T(8,128)}, u32[]{:S(2)}) copy-start(f32[1024,512,1]{1,0,2:T(8,128)} %constant.25) | copy-start | bytes 6291460
  63.0 7.0 %copy-start.9 = (f32[512,256]{0,1:T(8,128)S(1)}, f32[512,256]{0,1:T(8,128)}, u32[]{:S(2)}) copy-start(f32[512,256]{0,1:T(8,128)} %constant.21.clone) | copy-start | bytes 1572868
  63.0 7.1 %copy-start.10 = (f32[512,256]{0,1:T(8,128)S(1)}, f32[512,256]{0,1:T(8,128)}, u32[]{:S(2)}) copy-start(f32[512,256]{0,1:T(8,128)} %constant.20.clone) | copy-start | bytes 1572868
  70.1 1.2 copy-start.6
  75.5 1.2 copy-start.5
  76.8 2.1 %copy-start.7 = (f32[512,256]{1,0:T(8,128)S(1)}, f32[512,256]{1,0:T(8,128)}, u32[]{:S(2)}) copy-start(f32[512,256]{1,0:T(8,128)} %constant.29) | copy-start | bytes 1572868
  76.8 2.1 %copy-start.8 = (f32[512,256]{1,0:T(8,128)S(1)}, f32[512,256]{1,0:T(8,128)}, u32[]{:S(2)}) copy-start(f32[512,256]{1,0:T(8,128)} %constant.28) | copy-start | bytes 1572868
  78.9 1.6 %copy-start.2 = (f32[512,1024,1]{1,0,2:T(8,128)S(1)}, f32[512,1024,1]{1,0,2:T(8,128)}, u32[]{:S(2)}) copy-start(f32[512,1024,1]{1,0,2:T(8,128)} %constant.30) | copy-start | bytes 6291460
  117.6 1.0 copy-start.4
  117.6 1.0 copy-start.11
  117.7 26.3 %copy-start.12 = (f32[64]{0:T(128)S(1)}, f32[64]{0:T(128)}, u32[]{:S(2)}) copy-start(f32[64]{0:T(128)} %param.17) | copy-start | bytes 772

commit v2 on v1

v2 whole, which is shorter than its diff:
```python
import functools

import jax
import jax.numpy as jnp
import ml_dtypes
import numpy as np
from jax import lax
from jax.experimental import pallas as pl
from jax.experimental.pallas import tpu as pltpu
from jax.sharding import PartitionSpec as P

COLS = 256
SLOTS = 2
F32, BF16 = jnp.float32, jnp.bfloat16
DMA = pltpu.SemaphoreType.DMA


def turn(num, den):
    angle = 2.0 * np.pi * ((num % den) / den)
    return np.cos(angle), -np.sin(angle)


def halves(table):
    table = table.astype(np.float32)
    high = table.astype(ml_dtypes.bfloat16)
    low = (table - high.astype(np.float32)).astype(ml_dtypes.bfloat16)
    return high, low


def tables(rows, tile):
    size = rows * COLS
    freq = 4 * np.arange(rows, dtype=np.int64) + 1
    row, col = np.arange(rows, dtype=np.int64), np.arange(COLS, dtype=np.int64)
    f_re, f_im = turn(freq[:, None] * row[None, :], 4 * rows)
    t_re, t_im = turn(freq[:, None] * col[None, :], 4 * size)
    s_re, s_im = turn(col[:, None] * col[None, :], COLS)
    first = np.concatenate([f_re.reshape(-1, tile, rows), f_im.reshape(-1, tile, rows)], axis=1)
    second = np.block([[s_re, s_im], [-s_im, s_re]])
    back = np.block([[s_re, -s_im], [s_im, s_re]]) / size
    last = np.concatenate([f_re, f_im]).T
    twiddle = np.stack([t_re, t_im]).astype(np.float32)
    return (*halves(first), twiddle, *halves(second), *halves(back), *halves(last))


def split(value):
    high = value.astype(BF16)
    return high, (value - high.astype(F32)).astype(BF16)


def dot3(a_hi, a_lo, b_hi, b_lo):
    dot = functools.partial(jnp.dot, preferred_element_type=F32)
    return dot(a_hi, b_hi) + (dot(a_hi, b_lo) + dot(a_lo, b_hi))


def column(row):
    n = row.shape[1]
    eye = lax.broadcasted_iota(jnp.int32, (n, n), 0) == lax.broadcasted_iota(jnp.int32, (n, n), 1)
    return jnp.sum(jnp.where(eye, row, 0.0), axis=1, keepdims=True)


def kernel(
    n, groups, total_channels,
    gate_hbm, key_hbm, value_hbm, filter_hbm, skip_ref, gain_ref, *rest,
):
    tables_hbm, rest = rest[:9], rest[9:]
    out_ref, rest = rest[0], rest[1:]
    gate, key, value, filt = rest[:4]
    f_hi, f_lo, twiddle, s_hi, s_lo, b_hi, b_lo, l_hi, l_lo = tables_v = rest[4:13]
    (send_h, send_x, recv_h, recv_x, send_y, recv_y, x_hi, x_lo, mid_hi, mid_lo, spec_h, spec_x, d_hi, d_lo,
     branch, power, part, parts, in_sem, table_sem, out_sems, in_sems, ps_sem, pr_sem) = rest[13:]
    rows, wide = spec_h.shape
    tile = f_hi.shape[1] // 2
    channels, block = filt.shape
    ctx, ch = lax.axis_index("ctx"), lax.axis_index("ch")

    loads = [pltpu.make_async_copy(s, d, in_sem.at[i])
             for i, (s, d) in enumerate(((filter_hbm, filt), (key_hbm, key), (value_hbm, value), (gate_hbm, gate)))]
    for load in loads:
        load.start()
    table_loads = [pltpu.make_async_copy(s, d, table_sem.at[i]) for i, (s, d) in enumerate(zip(tables_hbm, tables_v))]
    for load in table_loads:
        load.start()

    barrier = pltpu.get_barrier_semaphore()

    def hello_ctx(i, _):
        pl.semaphore_signal(barrier, inc=1, device_id={"ctx": lax.rem(ctx + i, n)}, device_id_type=pl.DeviceIdType.MESH)
        return 0

    def hello_ch(i, _):
        pl.semaphore_signal(barrier, inc=1, device_id={"ch": lax.rem(ch + i, groups)},
                            device_id_type=pl.DeviceIdType.MESH)
        return 0

    lax.fori_loop(1, n, hello_ctx, 0)
    lax.fori_loop(1, groups, hello_ch, 0)

    def peer_of(i):
        if n % 8:
            return lax.rem(ctx + i, n)
        j = lax.rem(i, 8)
        odd = lax.rem(j, 2)
        step = odd * ((j + 1) // 2) + (1 - odd) * (8 - j // 2)
        fast = lax.rem(lax.rem(ctx, 8) + step, 8)
        slow = lax.rem(ctx // 8 + i // 8, n // 8)
        return slow * 8 + fast

    def exchange(src, dst, slot, kind):
        base = slot * n

        def one(i, _):
            p = peer_of(i)
            pltpu.make_async_remote_copy(
                src_ref=src.at[base + p], dst_ref=dst.at[base + ctx],
                send_sem=out_sems.at[kind, slot], recv_sem=in_sems.at[kind, slot],
                device_id={"ctx": p}, device_id_type=pl.DeviceIdType.MESH,
            ).start()
            return 0

        lax.fori_loop(1, n, one, 0)
        dst[pl.ds(base + ctx, 1)] = src[pl.ds(base + ctx, 1)]

    def arrived(dst, slot, kind):
        part = dst.at[pl.ds(0, n - 1)]
        pltpu.make_async_copy(part, part, in_sems.at[kind, slot]).wait()

    def lay_filter(slot, _):
        for c in range(0, n, 8):
            at = pl.ds(slot * n + c, 8)
            send_h[at] = filt[at].reshape(8, block // COLS, COLS)
        return 0

    def lay_driven(slot, _):
        for c in range(0, n, min(16, n)):
            at = pl.ds(slot * n + c, min(16, n))
            driven = key[at].astype(F32) * value[at].astype(F32)
            send_x[at] = driven.reshape(min(16, n), block // COLS, COLS)
        return 0

    def send_slot(slot, _):
        lay_filter(slot, 0)
        exchange(send_h, recv_h, slot, 0)
        lay_driven(slot, 0)
        exchange(send_x, recv_x, slot, 1)
        return 0

    for load in loads[:3]:
        load.wait()
    pl.semaphore_wait(barrier, (n - 1) + (groups - 1))
    lax.fori_loop(0, SLOTS, send_slot, 0)
    for load in table_loads:
        load.wait()

    def forward(src, slot, spec):
        x = src[pl.ds(slot * n, n)].reshape(rows, COLS)
        x_hi[...], x_lo[...] = split(x)

        def first(m, _):
            a = dot3(f_hi[m], f_lo[m], x_hi[...], x_lo[...])
            a_re, a_im = a[:tile], a[tile:]
            at = pl.ds(m * tile, tile)
            t_re, t_im = twiddle[0, at], twiddle[1, at]
            mid_hi[at, :COLS], mid_lo[at, :COLS] = split(a_re * t_re - a_im * t_im)
            mid_hi[at, COLS:], mid_lo[at, COLS:] = split(a_re * t_im + a_im * t_re)
            return 0

        def second(m, _):
            at = pl.ds(m * tile, tile)
            spec[at] = dot3(mid_hi[at], mid_lo[at], s_hi[...], s_lo[...])
            return 0

        lax.fori_loop(0, rows // tile, first, 0)
        lax.fori_loop(0, rows // tile, second, 0)

    def backward(slot):
        def first(m, _):
            at = pl.ds(m * tile, tile)
            x, h = spec_x[at], spec_h[at]
            x_re, x_im, h_re, h_im = x[:, :COLS], x[:, COLS:], h[:, :COLS], h[:, COLS:]
            p = jnp.concatenate([x_re * h_re - x_im * h_im, x_re * h_im + x_im * h_re], axis=1)
            c = dot3(*split(p), b_hi[...], b_lo[...])
            c_re, c_im = c[:, :COLS], c[:, COLS:]
            t_re, t_im = twiddle[0, at], twiddle[1, at]
            under = pl.ds(rows + m * tile, tile)
            d_hi[at], d_lo[at] = split(c_re * t_re + c_im * t_im)
            d_hi[under], d_lo[under] = split(c_im * t_re - c_re * t_im)
            return 0

        def second(m, _):
            at = pl.ds(m * tile, tile)
            y = dot3(l_hi[at], l_lo[at], d_hi[...], d_lo[...])
            blocks = tile // (block // COLS)
            send_y[pl.ds(slot * n + m * blocks, blocks)] = y.reshape(blocks, block // COLS, COLS)
            return 0

        lax.fori_loop(0, rows // tile, first, 0)
        lax.fori_loop(0, rows // tile, second, 0)

    def convolve(slot, _):
        arrived(recv_h, slot, 0)
        forward(recv_h, slot, spec_h)
        arrived(recv_x, slot, 1)
        forward(recv_x, slot, spec_x)
        backward(slot)
        exchange(send_y, recv_y, slot, 2)
        return 0

    lax.fori_loop(0, SLOTS, convolve, 0)
    loads[3].wait()
    skip, gain = column(skip_ref[...]), column(gain_ref[...])
    step = min(16, n)

    power[...] = jnp.zeros_like(power)
    for slot in range(SLOTS):
        arrived(recv_y, slot, 2)
        for c in range(slot * n, (slot + 1) * n, step):
            at = slice(c, c + step)
            driven = key[at].astype(F32) * value[at].astype(F32)
            conv = recv_y[at].reshape(step, block)
            b = gate[at].astype(F32) * (conv + skip[at] * driven)
            branch[at] = b
            square = b * b
            power[...] += sum(square[r:r + 8] for r in range(0, step, 8))
    part[...] = jnp.sum(power[...], axis=0, keepdims=True)

    def share(i, _):
        pltpu.make_async_remote_copy(
            src_ref=part, dst_ref=parts.at[ch], send_sem=ps_sem, recv_sem=pr_sem,
            device_id={"ch": lax.rem(ch + i, groups)}, device_id_type=pl.DeviceIdType.MESH,
        ).start()
        return 0

    lax.fori_loop(1, groups, share, 0)
    parts[pl.ds(ch, 1)] = part[...].reshape(1, 1, block)
    others = parts.at[pl.ds(0, groups - 1)]
    pltpu.make_async_copy(others, others, pr_sem).wait()
    mean = jnp.sum(parts[...], axis=0) / total_channels
    norm = lax.rsqrt(mean + 1e-6)
    for c in range(0, channels, step):
        at = slice(c, c + step)
        out_ref[at] = (branch[at] * gain[at] * norm).astype(BF16)

    pltpu.make_async_copy(others, others, ps_sem).wait()
    for kind, src in enumerate((send_h, send_x, send_y)):
        for slot in range(SLOTS):
            sent = src.at[pl.ds(0, n - 1)]
            pltpu.make_async_copy(sent, sent, out_sems.at[kind, slot]).wait()


def solution(mesh):
    n, groups = mesh.shape["ctx"], mesh.shape["ch"]

    def body(gate_in, key_in, value_in, long_filter, skip_weight, norm_gain):
        channels, block = gate_in.shape
        rows = n * block // COLS
        tile = min(128, rows)
        blocks = pltpu.VMEM((channels, block // COLS, COLS), F32)
        constants = tables(rows, tile)
        vmem, anywhere = pl.BlockSpec(memory_space=pltpu.VMEM), pl.BlockSpec(memory_space=pl.ANY)
        return pl.pallas_call(
            functools.partial(kernel, n, groups, channels * groups),
            out_shape=jax.ShapeDtypeStruct((channels, block), BF16),
            in_specs=[anywhere] * 4 + [vmem] * 2 + [anywhere] * len(constants),
            out_specs=vmem,
            scratch_shapes=[
                pltpu.VMEM((channels, block), BF16),
                pltpu.VMEM((channels, block), BF16),
                pltpu.VMEM((channels, block), BF16),
                pltpu.VMEM((channels, block), F32),
                *[pltpu.VMEM(c.shape, c.dtype) for c in constants],
                blocks, blocks, blocks, blocks, blocks, blocks,
                pltpu.VMEM((rows, COLS), BF16), pltpu.VMEM((rows, COLS), BF16),
                pltpu.VMEM((rows, 2 * COLS), BF16), pltpu.VMEM((rows, 2 * COLS), BF16),
                pltpu.VMEM((rows, 2 * COLS), F32), pltpu.VMEM((rows, 2 * COLS), F32),
                pltpu.VMEM((2 * rows, COLS), BF16), pltpu.VMEM((2 * rows, COLS), BF16),
                pltpu.VMEM((channels, block), F32),
                pltpu.VMEM((8, block), F32),
                pltpu.VMEM((1, block), F32),
                pltpu.VMEM((groups, 1, block), F32),
                DMA((4,)), DMA((len(constants),)),
                DMA((3, SLOTS)), DMA((3, SLOTS)), DMA, DMA,
            ],
            compiler_params=pltpu.CompilerParams(
                collective_id=0, has_side_effects=True, vmem_limit_bytes=50 * 1024 * 1024),
            cost_estimate=pl.CostEstimate(flops=10**10, bytes_accessed=12 * 2**20, transcendentals=4096),
        )(gate_in, key_in, value_in, long_filter, skip_weight.reshape(1, channels), norm_gain.reshape(1, channels),
          *[jnp.asarray(c) for c in constants])

    specs = (P("ch", "ctx"), P("ch", "ctx"), P("ch", "ctx"), P("ch", "ctx"), P("ch"), P("ch"))
    return jax.shard_map(body, mesh=mesh, in_specs=specs, out_specs=P("ch", "ctx"), check_vma=False)
```

time: 147 us -> 94.6 us (0.64)
  blocking collectives: 117 us -> 0 us
  Pallas kernels: 0 us -> 86.5 us
  matrix products: 16.8 us -> 0 us
  other arithmetic: 3.41 us -> 0 us
    all_to_all x2 -> x0, blocking collectives: 92.1 us -> none  [the longest x1 58.9 us: body(): both = lax.all_to_all(both, 'ctx', split_axis=2, concat_axis=2, tiled=True)]
    pallas_call x0 -> x1, Pallas kernels: none -> 86.5 us  [body(): pl.pallas_call(functools.partial(kernel, n, groups, channels * groups), o...]
    psum x1 -> x0, blocking collectives: 25 us -> none  [body(): total = lax.psum(jnp.sum(branch * branch, axis=0), 'ch')]
    dot_general x4 -> x0, matrix products: 16.8 us -> none  [the longest x1 7.03 us: body(): a = jnp.einsum('kr,brl->bkl', first, both, precision=HIGH)]
    unnamed x29 -> x17, local copies, waits for them, and re-layouts: 6.72 us -> 7.71 us
where the time goes in v2:
time: 94.6 us; the launch traced here: 94.2 us
  Pallas kernels  86.5 us (91%)
  local copies, waits for them, and re-layouts  7.71 us (8%)
    pallas_call x1, Pallas kernels, body(): pl.pallas_call(functools.partial(kernel, n, groups, channels * groups), o...  86.5 us
    unnamed x17, local copies, waits for them, and re-layouts  7.71 us

profile of v2, /device:TPU:1, one launch (start us, length us, event | category | flops | bytes accessed | tf_op | source)
XLA Modules:
  0.0 94.2 jit_solution(18152701866332091143)
XLA Ops:
  0.0 0.0 copy-start.3
  0.0 0.0 copy-start.4
  0.0 0.7 copy-done.3
  0.7 0.0 copy-done.4
  0.7 0.0 copy-start
  0.7 1.0 %copy-done = bf16[64,4096]{1,0:T(8,128)(2,1)S(1)} copy-done((bf16[64,4096]{1,0:T(8,128)(2,1)S(1)}, bf16[64,4096]{1,0:T(8,128)(2,1)}, u32[]{:S(2)}) %copy-start) | copy-done | bytes 524312
  1.7 0.0 copy-start.1
  1.7 1.0 %copy-done.1 = bf16[64,4096]{1,0:T(8,128)(2,1)S(1)} copy-done((bf16[64,4096]{1,0:T(8,128)(2,1)S(1)}, bf16[64,4096]{1,0:T(8,128)(2,1)}, u32[]{:S(2)}) %copy-start.1) | copy-done | bytes 524312
  2.8 0.0 copy-start.2
  2.8 1.0 %copy-done.2 = bf16[64,4096]{1,0:T(8,128)(2,1)S(1)} copy-done((bf16[64,4096]{1,0:T(8,128)(2,1)S(1)}, bf16[64,4096]{1,0:T(8,128)(2,1)}, u32[]{:S(2)}) %copy-start.2) | copy-done | bytes 524312
  3.8 0.0 copy-start.5
  3.8 1.0 %copy-done.5 = bf16[512,512]{1,0:T(8,128)(2,1)S(1)} copy-done((bf16[512,512]{1,0:T(8,128)(2,1)S(1)}, bf16[512,512]{1,0:T(8,128)(2,1)}, u32[]{:S(2)}) %copy-start.5) | copy-done | bytes 524312
  4.8 0.0 copy-start.6
  4.8 1.0 %copy-done.6 = bf16[512,512]{1,0:T(8,128)(2,1)S(1)} copy-done((bf16[512,512]{1,0:T(8,128)(2,1)S(1)}, bf16[512,512]{1,0:T(8,128)(2,1)}, u32[]{:S(2)}) %copy-start.6) | copy-done | bytes 524312
  5.9 0.0 copy-start.7
  5.9 1.0 %copy-done.7 = bf16[512,512]{1,0:T(8,128)(2,1)S(1)} copy-done((bf16[512,512]{1,0:T(8,128)(2,1)S(1)}, bf16[512,512]{1,0:T(8,128)(2,1)}, u32[]{:S(2)}) %copy-start.7) | copy-done | bytes 524312
  6.9 86.5 %shard_map.145 = bf16[64,4096]{1,0:T(8,128)(2,1)S(1)} custom-call(bf16[64,4096]{1,0:T(8,128)(2,1)S(1)} %copy-done, bf16[64,4096]{1,0:T(8,128)(2,1)S(1)} %copy-done.1, bf16[64,4096]{1,0:T(8,128)(2,1)S(1)} %copy-done.2, f32[64,4096]{1,0:T(8,128)} %filter_hbm.1, f32[1,64]{1,0:T(1,128)S(1)} %bitcast.2, f32[1,64]{1,0:T(1,128)S(1)} %bitcast.3, ...), custom_call_target="tpu_custom_call" | custom-call | flops 10000000000 | bytes 12582912 | tf_op jit(solution)/shard_map/pallas_call | solution.py:260
  93.4 0.8 copy.17
Async XLA Ops:
  0.0 0.7 copy-start.3
  0.0 0.7 copy-start.4
  0.7 1.0 %copy-start = (bf16[64,4096]{1,0:T(8,128)(2,1)S(1)}, bf16[64,4096]{1,0:T(8,128)(2,1)}, u32[]{:S(2)}) copy-start(bf16[64,4096]{1,0:T(8,128)(2,1)} %gate_hbm.1) | copy-start | bytes 1572868
  1.7 1.0 %copy-start.1 = (bf16[64,4096]{1,0:T(8,128)(2,1)S(1)}, bf16[64,4096]{1,0:T(8,128)(2,1)}, u32[]{:S(2)}) copy-start(bf16[64,4096]{1,0:T(8,128)(2,1)} %key_hbm.1) | copy-start | bytes 1572868
  2.8 1.0 %copy-start.2 = (bf16[64,4096]{1,0:T(8,128)(2,1)S(1)}, bf16[64,4096]{1,0:T(8,128)(2,1)}, u32[]{:S(2)}) copy-start(bf16[64,4096]{1,0:T(8,128)(2,1)} %value_hbm.1) | copy-start | bytes 1572868
  3.8 1.0 %copy-start.5 = (bf16[512,512]{1,0:T(8,128)(2,1)S(1)}, bf16[512,512]{1,0:T(8,128)(2,1)}, u32[]{:S(2)}) copy-start(bf16[512,512]{1,0:T(8,128)(2,1)} %constant.23.clone.rest_5_) | copy-start | bytes 1572868
  4.8 1.0 %copy-start.6 = (bf16[512,512]{1,0:T(8,128)(2,1)S(1)}, bf16[512,512]{1,0:T(8,128)(2,1)}, u32[]{:S(2)}) copy-start(bf16[512,512]{1,0:T(8,128)(2,1)} %constant.22.clone.rest_4_) | copy-start | bytes 1572868
  5.9 1.0 %copy-start.7 = (bf16[512,512]{1,0:T(8,128)(2,1)S(1)}, bf16[512,512]{1,0:T(8,128)(2,1)}, u32[]{:S(2)}) copy-start(bf16[512,512]{1,0:T(8,128)(2,1)} %constant.21.clone.rest_3_) | copy-start | bytes 1572868

commit v3 on v2

v3 whole, which is shorter than its diff:
```python
import functools

import jax
import jax.numpy as jnp
import ml_dtypes
import numpy as np
from jax import lax
from jax.experimental import pallas as pl
from jax.experimental.pallas import tpu as pltpu
from jax.sharding import PartitionSpec as P

COLS = 256
SLOTS = 2
F32, BF16 = jnp.float32, jnp.bfloat16
VMEM_LIMIT = 63 * 2**20
DMA = pltpu.SemaphoreType.DMA


def turn(num, den):
    angle = 2.0 * np.pi * ((num % den) / den)
    return np.cos(angle), -np.sin(angle)


def halves(table):
    table = table.astype(np.float32)
    high = table.astype(ml_dtypes.bfloat16)
    low = (table - high.astype(np.float32)).astype(ml_dtypes.bfloat16)
    return high, low


def tables(rows, tile):
    size = rows * COLS
    freq = 4 * np.arange(rows, dtype=np.int64) + 1
    row, col = np.arange(rows, dtype=np.int64), np.arange(COLS, dtype=np.int64)
    f_re, f_im = turn(freq[:, None] * row[None, :], 4 * rows)
    t_re, t_im = turn(freq[:, None] * col[None, :], 4 * size)
    s_re, s_im = turn(col[:, None] * col[None, :], COLS)
    first = np.concatenate([f_re.reshape(-1, tile, rows), f_im.reshape(-1, tile, rows)], axis=1).reshape(2 * rows, rows)
    second = np.block([[s_re, s_im], [-s_im, s_re]])
    back = np.block([[s_re, -s_im], [s_im, s_re]]) / size
    last = np.concatenate([f_re.T, f_im.T])
    twiddle = np.stack([t_re, t_im]).astype(np.float32)
    wide = max(rows, 2 * COLS)
    stacked = np.concatenate([np.pad(t, ((0, 0), (0, wide - t.shape[1]))) for t in (first, last, second, back)])
    return np.stack(halves(stacked)), twiddle


def split(value):
    high = value.astype(BF16)
    return high, (value - high.astype(F32)).astype(BF16)


def dot3(a_hi, a_lo, b_hi, b_lo):
    dot = functools.partial(jnp.dot, preferred_element_type=F32)
    return dot(a_hi, b_hi) + (dot(a_hi, b_lo) + dot(a_lo, b_hi))


def column(row):
    n = row.shape[1]
    eye = lax.broadcasted_iota(jnp.int32, (n, n), 0) == lax.broadcasted_iota(jnp.int32, (n, n), 1)
    return jnp.sum(jnp.where(eye, row, 0.0), axis=1, keepdims=True)


def kernel(
    n, groups, total_channels,
    gate_hbm, key_hbm, value_hbm, filter_hbm, skip_hbm, gain_hbm, *rest,
):
    tables_hbm, (out_hbm, *rest) = rest[:2], rest[2:]
    gate, key, value, filt, skip_ref, gain_ref = rest[:6]
    matrices, twiddle = tables_v = rest[6:8]
    (send_h, send_x, recv_h, recv_x, send_y, recv_y, x_hi, x_lo, mid_hi, mid_lo, spec_h, spec_x, d_hi, d_lo,
     gated, direct, scaled, power, part, parts, mixed,
     load_sems, table_sem, out_sems, in_sems, back_sems, ps_sem, pr_sem, store_sem) = rest[8:]
    rows, wide = spec_h.shape
    tile = min(128, rows)
    f_at, l_at, s_at, b_at = 0, 2 * rows, 4 * rows, 4 * rows + wide
    channels, block = gate.shape
    ctx, ch = lax.axis_index("ctx"), lax.axis_index("ch")
    step = min(16, n)
    ring = min(8, n)
    mesh_id = pl.DeviceIdType.MESH

    def half(ref, slot):
        return ref.at[pl.ds(slot * n, n)]

    pairs = [(half(filter_hbm, 0), half(filt, 0)), (key_hbm, key), (value_hbm, value), (half(filter_hbm, 1), half(filt, 1)),
             (gate_hbm, gate), (skip_hbm, skip_ref), (gain_hbm, gain_ref)]
    loads = [pltpu.make_async_copy(s, d, load_sems.at[i]) for i, (s, d) in enumerate(pairs)]
    table_loads = [pltpu.make_async_copy(s, d, table_sem.at[i]) for i, (s, d) in enumerate(zip(tables_hbm, tables_v))]
    for load in loads + table_loads:
        load.start()

    barrier = pltpu.get_barrier_semaphore()

    def hello_ctx(i, _):
        pl.semaphore_signal(barrier, inc=1, device_id={"ctx": lax.rem(ctx + i, n)}, device_id_type=mesh_id)
        return 0

    def hello_ch(i, _):
        pl.semaphore_signal(barrier, inc=1, device_id={"ch": lax.rem(ch + i, groups)}, device_id_type=mesh_id)
        return 0

    lax.fori_loop(1, n, hello_ctx, 0)
    lax.fori_loop(1, groups, hello_ch, 0)

    def peer_of(i):
        j = lax.rem(i, ring)
        odd = lax.rem(j, 2)
        move = odd * ((j + 1) // 2) + (1 - odd) * (ring - j // 2)
        fast = lax.rem(lax.rem(ctx, ring) + move, ring)
        slow = lax.rem(ctx // ring + i // ring, n // ring)
        return slow * ring + fast

    def exchange(src, dst, slot, kind):
        base = slot * n

        def one(i, _):
            p = peer_of(i)
            arrival = back_sems.at[slot, i // ring] if kind == 2 else in_sems.at[kind, slot]
            pltpu.make_async_remote_copy(
                src_ref=src.at[base + p], dst_ref=dst.at[base + ctx], send_sem=out_sems.at[kind],
                recv_sem=arrival, device_id={"ctx": p}, device_id_type=mesh_id,
            ).start()
            return 0

        lax.fori_loop(1, n, one, 0)
        dst[pl.ds(base + ctx, 1)] = src[pl.ds(base + ctx, 1)]

    def landed(dst, count, sem):
        some = dst.at[pl.ds(0, count)]
        pltpu.make_async_copy(some, some, sem).wait()

    def lay_filter(slot):
        for c in range(0, n, 8):
            at = pl.ds(slot * n + c, 8)
            send_h[at] = filt[at].reshape(8, block // COLS, COLS)

    def lay_driven(slot):
        for c in range(0, n, step):
            at = pl.ds(slot * n + c, step)
            driven = key[at].astype(F32) * value[at].astype(F32)
            send_x[at] = driven.reshape(step, block // COLS, COLS)

    for load in loads[:4]:
        load.wait()
    pl.semaphore_wait(barrier, (n - 1) + (groups - 1))
    for slot in range(SLOTS):
        lay_filter(slot)
        exchange(send_h, recv_h, slot, 0)
        lay_driven(slot)
        exchange(send_x, recv_x, slot, 1)
    for load in loads[4:]:
        load.wait()

    skip, gain = column(skip_ref[...]), column(gain_ref[...])
    for c in range(0, channels, step):
        at = slice(c, c + step)
        gated[at] = gate[at].astype(F32)
        direct[at] = skip[at] * (key[at].astype(F32) * value[at].astype(F32))
    for load in table_loads:
        load.wait()

    def matrix(start, count, width):
        at = pl.ds(start, count)
        return matrices[0, at, :width], matrices[1, at, :width]

    def forward(src, slot, spec):
        x = src[pl.ds(slot * n, n)].reshape(rows, COLS)
        x_hi[...], x_lo[...] = split(x)

        def first(m, _):
            a = dot3(*matrix(f_at + m * 2 * tile, 2 * tile, rows), x_hi[...], x_lo[...])
            a_re, a_im = a[:tile], a[tile:]
            at = pl.ds(m * tile, tile)
            t_re, t_im = twiddle[0, at], twiddle[1, at]
            mid_hi[at, :COLS], mid_lo[at, :COLS] = split(a_re * t_re - a_im * t_im)
            mid_hi[at, COLS:], mid_lo[at, COLS:] = split(a_re * t_im + a_im * t_re)
            return 0

        def second(m, _):
            at = pl.ds(m * tile, tile)
            spec[at] = dot3(mid_hi[at], mid_lo[at], *matrix(s_at, wide, wide))
            return 0

        lax.fori_loop(0, rows // tile, first, 0)
        lax.fori_loop(0, rows // tile, second, 0)

    def backward(slot):
        def first(m, _):
            at = pl.ds(m * tile, tile)
            x, h = spec_x[at], spec_h[at]
            x_re, x_im, h_re, h_im = x[:, :COLS], x[:, COLS:], h[:, :COLS], h[:, COLS:]
            p = jnp.concatenate([x_re * h_re - x_im * h_im, x_re * h_im + x_im * h_re], axis=1)
            c = dot3(*split(p), *matrix(b_at, wide, wide))
            c_re, c_im = c[:, :COLS], c[:, COLS:]
            t_re, t_im = twiddle[0, at], twiddle[1, at]
            under = pl.ds(rows + m * tile, tile)
            d_hi[at], d_lo[at] = split(c_re * t_re + c_im * t_im)
            d_hi[under], d_lo[under] = split(c_im * t_re - c_re * t_im)
            return 0

        def second(m, _):
            at = pl.ds(m * tile, tile)
            y = dot3(*matrix(l_at + m * tile, tile, rows), d_hi[:rows], d_lo[:rows])
            y += dot3(*matrix(l_at + rows + m * tile, tile, rows), d_hi[rows:], d_lo[rows:])
            blocks = tile // (block // COLS)
            send_y[pl.ds(slot * n + m * blocks, blocks)] = y.reshape(blocks, block // COLS, COLS)
            return 0

        lax.fori_loop(0, rows // tile, first, 0)
        lax.fori_loop(0, rows // tile, second, 0)

    def convolve(slot, _):
        landed(recv_h, n - 1, in_sems.at[0, slot])
        forward(recv_h, slot, spec_h)
        landed(recv_x, n - 1, in_sems.at[1, slot])
        forward(recv_x, slot, spec_x)
        backward(slot)
        exchange(send_y, recv_y, slot, 2)
        return 0

    lax.fori_loop(0, SLOTS, convolve, 0)

    power[...] = jnp.zeros_like(power)
    for slot in range(SLOTS):
        for away in range(n // ring):
            landed(recv_y, ring - (away == 0), back_sems.at[slot, away])
            owner = lax.rem(ctx // ring + (n // ring - away), n // ring)
            at = pl.ds(pl.multiple_of(slot * n + owner * ring, ring), ring)
            conv = recv_y[at].reshape(ring, block)
            branch = gated[at] * (conv + direct[at])
            scaled[at] = branch
            power[...] += branch * branch
    part[...] = jnp.sum(power[...], axis=0, keepdims=True)

    def share(i, _):
        pltpu.make_async_remote_copy(
            src_ref=part, dst_ref=parts.at[ch], send_sem=ps_sem, recv_sem=pr_sem,
            device_id={"ch": lax.rem(ch + i, groups)}, device_id_type=mesh_id,
        ).start()
        return 0

    lax.fori_loop(1, groups, share, 0)
    parts[pl.ds(ch, 1)] = part[...].reshape(1, 1, block)
    landed(parts, groups - 1, pr_sem)
    mean = jnp.sum(parts[...], axis=0) / total_channels
    norm = lax.rsqrt(mean + 1e-6)
    for c in range(0, channels, step):
        at = slice(c, c + step)
        mixed[at] = (scaled[at] * gain[at] * norm).astype(BF16)
        pltpu.make_async_copy(mixed.at[at], out_hbm.at[at], store_sem).start()

    landed(parts, groups - 1, ps_sem)
    for kind, src in enumerate((send_h, send_x, send_y)):
        landed(src, SLOTS * (n - 1), out_sems.at[kind])
    pltpu.make_async_copy(mixed, out_hbm, store_sem).wait()


def solution(mesh):
    n, groups = mesh.shape["ctx"], mesh.shape["ch"]

    def body(gate_in, key_in, value_in, long_filter, skip_weight, norm_gain):
        channels, block = gate_in.shape
        rows = n * block // COLS
        tile = min(128, rows)
        blocks = pltpu.VMEM((channels, block // COLS, COLS), F32)
        half, full = pltpu.VMEM((channels, block), BF16), pltpu.VMEM((channels, block), F32)
        constants = tables(rows, tile)
        hbm = pl.BlockSpec(memory_space=pltpu.HBM)
        return pl.pallas_call(
            functools.partial(kernel, n, groups, channels * groups),
            out_shape=jax.ShapeDtypeStruct((channels, block), BF16),
            in_specs=[hbm] * (6 + len(constants)),
            out_specs=hbm,
            scratch_shapes=[
                half, half, half, full,
                pltpu.VMEM((1, channels), F32), pltpu.VMEM((1, channels), F32),
                *[pltpu.VMEM(c.shape, c.dtype) for c in constants],
                blocks, blocks, blocks, blocks, blocks, blocks,
                pltpu.VMEM((rows, COLS), BF16), pltpu.VMEM((rows, COLS), BF16),
                pltpu.VMEM((rows, 2 * COLS), BF16), pltpu.VMEM((rows, 2 * COLS), BF16),
                pltpu.VMEM((rows, 2 * COLS), F32), pltpu.VMEM((rows, 2 * COLS), F32),
                pltpu.VMEM((2 * rows, COLS), BF16), pltpu.VMEM((2 * rows, COLS), BF16),
                full, full, full,
                pltpu.VMEM((min(8, n), block), F32),
                pltpu.VMEM((1, block), F32),
                pltpu.VMEM((groups, 1, block), F32),
                half,
                DMA((7,)), DMA((len(constants),)), DMA((3,)), DMA((2, SLOTS)), DMA((SLOTS, n // min(8, n))),
                DMA, DMA, DMA,
            ],
            compiler_params=pltpu.CompilerParams(
                collective_id=0, has_side_effects=True, vmem_limit_bytes=VMEM_LIMIT),
            cost_estimate=pl.CostEstimate(flops=10**10, bytes_accessed=12 * 2**20, transcendentals=4096),
        )(gate_in, key_in, value_in, long_filter, skip_weight.reshape(1, channels), norm_gain.reshape(1, channels),
          *[jnp.asarray(c) for c in constants])

    specs = (P("ch", "ctx"), P("ch", "ctx"), P("ch", "ctx"), P("ch", "ctx"), P("ch"), P("ch"))
    return jax.shard_map(body, mesh=mesh, in_specs=specs, out_specs=P("ch", "ctx"), check_vma=False)
```

time: 94.6 us -> 88.7 us (0.938)
  local copies, waits for them, and re-layouts: 7.71 us -> 1.87 us
    unnamed x17 -> x1, local copies, waits for them, and re-layouts: 7.71 us -> 1.87 us
where the time goes in v3:
time: 88.7 us; the launch traced here: 88.6 us
  Pallas kernels  86.8 us (98%)
  local copies, waits for them, and re-layouts  1.87 us (2%)
    pallas_call x1, Pallas kernels, body(): pl.pallas_call(functools.partial(kernel, n, groups, channels * groups), o...  86.8 us
    unnamed x1, local copies, waits for them, and re-layouts  1.87 us

profile of v3, /device:TPU:1, one launch (start us, length us, event | category | flops | bytes accessed | tf_op | source)
XLA Modules:
  0.0 88.6 jit_solution(17775561720267903272)
XLA Ops:
  0.0 86.8 %shard_map.82 = bf16[64,4096]{1,0:T(8,128)(2,1)} custom-call(bf16[64,4096]{1,0:T(8,128)(2,1)} %gate_hbm.1, bf16[64,4096]{1,0:T(8,128)(2,1)} %key_hbm.1, bf16[64,4096]{1,0:T(8,128)(2,1)} %value_hbm.1, f32[64,4096]{1,0:T(8,128)} %filter_hbm.1, f32[1,64]{1,0:T(1,128)} %bitcast.2, f32[1,64]{1,0:T(1,128)} %bitcast.3, ...), custom_call_target="tpu_custom_call" | custom-call | flops 10000000000 | bytes 12582912 | tf_op jit(solution)/shard_map/pallas_call | solution.py:270
  86.8 1.9 %copy.10 = bf16[64,4096]{1,0:T(8,128)(2,1)} copy(bf16[64,4096]{1,0:T(8,128)(2,1)} %shard_map.82) | data formatting | bytes 1048576

commit v4 on v3

--- a/solution.py
+++ b/solution.py
@@ -13,6 +13,7 @@
 SLOTS = 2
 F32, BF16 = jnp.float32, jnp.bfloat16
 VMEM_LIMIT = 63 * 2**20
+EARLY = (0, 24, 8, 16, 25, 1, 9, 17, 26, 2, 10, 18, 27, 3, 11, 19)
 DMA = pltpu.SemaphoreType.DMA
 
 
@@ -87,7 +88,7 @@
              (gate_hbm, gate), (skip_hbm, skip_ref), (gain_hbm, gain_ref)]
     loads = [pltpu.make_async_copy(s, d, load_sems.at[i]) for i, (s, d) in enumerate(pairs)]
     table_loads = [pltpu.make_async_copy(s, d, table_sem.at[i]) for i, (s, d) in enumerate(zip(tables_hbm, tables_v))]
-    for load in loads + table_loads:
+    for load in loads[:4]:
         load.start()
 
     barrier = pltpu.get_barrier_semaphore()
@@ -111,18 +112,28 @@
         slow = lax.rem(ctx // ring + i // ring, n // ring)
         return slow * ring + fast
 
-    def exchange(src, dst, slot, kind):
+    def exchange(src, dst, slot, kind, first=()):
         base = slot * n
 
-        def one(i, _):
-            p = peer_of(i)
-            arrival = back_sems.at[slot, i // ring] if kind == 2 else in_sems.at[kind, slot]
+        def push(p, group):
+            arrival = back_sems.at[slot, group] if kind == 2 else in_sems.at[kind, slot]
             pltpu.make_async_remote_copy(
                 src_ref=src.at[base + p], dst_ref=dst.at[base + ctx], send_sem=out_sems.at[kind],
                 recv_sem=arrival, device_id={"ctx": p}, device_id_type=mesh_id,
             ).start()
-            return 0
-
+
+        def one(i, _):
+            p = peer_of(i)
+            if first:
+                later = functools.reduce(jnp.logical_and, [p != q for q in first])
+                pl.when(later)(lambda: push(p, i // ring))
+            else:
+                push(p, i // ring)
+            return 0
+
+        for q in first:
+            group = lax.rem(q // ring + n // ring - ctx // ring, n // ring)
+            pl.when(ctx != q)(lambda q=q, group=group: push(q, group))
         lax.fori_loop(1, n, one, 0)
         dst[pl.ds(base + ctx, 1)] = src[pl.ds(base + ctx, 1)]
 
@@ -141,14 +152,21 @@
             driven = key[at].astype(F32) * value[at].astype(F32)
             send_x[at] = driven.reshape(step, block // COLS, COLS)
 
-    for load in loads[:4]:
-        load.wait()
+    loads[0].wait()
     pl.semaphore_wait(barrier, (n - 1) + (groups - 1))
-    for slot in range(SLOTS):
-        lay_filter(slot)
-        exchange(send_h, recv_h, slot, 0)
-        lay_driven(slot)
-        exchange(send_x, recv_x, slot, 1)
+    lay_filter(0)
+    exchange(send_h, recv_h, 0, 0)
+    loads[1].wait()
+    loads[2].wait()
+    lay_driven(0)
+    exchange(send_x, recv_x, 0, 1)
+    loads[3].wait()
+    lay_filter(1)
+    exchange(send_h, recv_h, 1, 0)
+    lay_driven(1)
+    exchange(send_x, recv_x, 1, 1)
+    for load in loads[4:] + table_loads:
+        load.start()
     for load in loads[4:]:
         load.wait()
 
@@ -210,16 +228,17 @@
         lax.fori_loop(0, rows // tile, first, 0)
         lax.fori_loop(0, rows // tile, second, 0)
 
-    def convolve(slot, _):
+    def convolve(slot):
         landed(recv_h, n - 1, in_sems.at[0, slot])
         forward(recv_h, slot, spec_h)
         landed(recv_x, n - 1, in_sems.at[1, slot])
         forward(recv_x, slot, spec_x)
         backward(slot)
-        exchange(send_y, recv_y, slot, 2)
-        return 0
-
-    lax.fori_loop(0, SLOTS, convolve, 0)
+
+    early = tuple(q for q in EARLY if q < n)
+    for slot in range(SLOTS):
+        convolve(slot)
+        exchange(send_y, recv_y, slot, 2, early if slot == SLOTS - 1 else ())
 
     power[...] = jnp.zeros_like(power)
     for slot in range(SLOTS):

time: 88.7 us -> 86.7 us (0.977)
  the two profiles are of different devices: /device:TPU:1 before, /device:TPU:65 now
where the time goes in v4:
time: 86.7 us; the launch traced here: 86.6 us
  Pallas kernels  84.7 us (98%)
  local copies, waits for them, and re-layouts  1.87 us (2%)
    pallas_call x1, Pallas kernels, body(): pl.pallas_call(functools.partial(kernel, n, groups, channels * groups), o...  84.7 us
    unnamed x1, local copies, waits for them, and re-layouts  1.87 us

profile of v4, /device:TPU:65, one launch (start us, length us, event | category | flops | bytes accessed | tf_op | source)
XLA Modules:
  0.0 86.6 jit_solution(1059839421168795040)
XLA Ops:
  0.0 84.7 %shard_map.82 = bf16[64,4096]{1,0:T(8,128)(2,1)} custom-call(bf16[64,4096]{1,0:T(8,128)(2,1)} %gate_hbm.1, bf16[64,4096]{1,0:T(8,128)(2,1)} %key_hbm.1, bf16[64,4096]{1,0:T(8,128)(2,1)} %value_hbm.1, f32[64,4096]{1,0:T(8,128)} %filter_hbm.1, f32[1,64]{1,0:T(1,128)} %bitcast.2, f32[1,64]{1,0:T(1,128)} %bitcast.3, ...), custom_call_target="tpu_custom_call" | custom-call | flops 10000000000 | bytes 12582912 | tf_op jit(solution)/shard_map/pallas_call | solution.py:289
  84.7 1.9 %copy.10 = bf16[64,4096]{1,0:T(8,128)(2,1)} copy(bf16[64,4096]{1,0:T(8,128)(2,1)} %shard_map.82) | data formatting | bytes 1048576

commit v5 on v4

--- a/solution.py
+++ b/solution.py
@@ -13,7 +13,7 @@
 SLOTS = 2
 F32, BF16 = jnp.float32, jnp.bfloat16
 VMEM_LIMIT = 63 * 2**20
-EARLY = (0, 24, 8, 16, 25, 1, 9, 17, 26, 2, 10, 18, 27, 3, 11, 19)
+EARLY = (0, 24, 8, 1, 16, 25, 9, 2, 17, 10, 26, 18, 3, 11, 27, 19)
 DMA = pltpu.SemaphoreType.DMA
 
 

time: 86.7 us -> 86.1 us (level)
  the two profiles are of different devices: /device:TPU:65 before, /device:TPU:81 now
where the time goes in v5:
time: 86.1 us; the launch traced here: 85.9 us
  Pallas kernels  84 us (98%)
  local copies, waits for them, and re-layouts  1.87 us (2%)
    pallas_call x1, Pallas kernels, body(): pl.pallas_call(functools.partial(kernel, n, groups, channels * groups), o...  84 us
    unnamed x1, local copies, waits for them, and re-layouts  1.87 us

profile of v5, /device:TPU:81, one launch (start us, length us, event | category | flops | bytes accessed | tf_op | source)
XLA Modules:
  0.0 85.9 jit_solution(9854435454720937541)
XLA Ops:
  0.0 84.0 %shard_map.82 = bf16[64,4096]{1,0:T(8,128)(2,1)} custom-call(bf16[64,4096]{1,0:T(8,128)(2,1)} %gate_hbm.1, bf16[64,4096]{1,0:T(8,128)(2,1)} %key_hbm.1, bf16[64,4096]{1,0:T(8,128)(2,1)} %value_hbm.1, f32[64,4096]{1,0:T(8,128)} %filter_hbm.1, f32[1,64]{1,0:T(1,128)} %bitcast.2, f32[1,64]{1,0:T(1,128)} %bitcast.3, ...), custom_call_target="tpu_custom_call" | custom-call | flops 10000000000 | bytes 12582912 | tf_op jit(solution)/shard_map/pallas_call | solution.py:289
  84.0 1.9 %copy.10 = bf16[64,4096]{1,0:T(8,128)(2,1)} copy(bf16[64,4096]{1,0:T(8,128)(2,1)} %shard_map.82) | data formatting | bytes 1048576

commit v6 on v5

--- a/solution.py
+++ b/solution.py
@@ -12,7 +12,7 @@
 COLS = 256
 SLOTS = 2
 F32, BF16 = jnp.float32, jnp.bfloat16
-VMEM_LIMIT = 63 * 2**20
+VMEM_LIMIT = 53 * 2**20
 EARLY = (0, 24, 8, 1, 16, 25, 9, 2, 17, 10, 26, 18, 3, 11, 27, 19)
 DMA = pltpu.SemaphoreType.DMA
 
@@ -64,14 +64,14 @@
 
 def kernel(
     n, groups, total_channels,
-    gate_hbm, key_hbm, value_hbm, filter_hbm, skip_hbm, gain_hbm, *rest,
+    gate_hbm, key_hbm, value_hbm, filter_hbm, weights_hbm, *rest,
 ):
     tables_hbm, (out_hbm, *rest) = rest[:2], rest[2:]
-    gate, key, value, filt, skip_ref, gain_ref = rest[:6]
-    matrices, twiddle = tables_v = rest[6:8]
+    gate, key, value, filt, weights = rest[:5]
+    matrices, twiddle = tables_v = rest[5:7]
     (send_h, send_x, recv_h, recv_x, send_y, recv_y, x_hi, x_lo, mid_hi, mid_lo, spec_h, spec_x, d_hi, d_lo,
      gated, direct, scaled, power, part, parts, mixed,
-     load_sems, table_sem, out_sems, in_sems, back_sems, ps_sem, pr_sem, store_sem) = rest[8:]
+     load_sems, table_sem, out_sems, in_sems, back_sems, ps_sem, pr_sem, store_sem) = rest[7:]
     rows, wide = spec_h.shape
     tile = min(128, rows)
     f_at, l_at, s_at, b_at = 0, 2 * rows, 4 * rows, 4 * rows + wide
@@ -85,7 +85,7 @@
         return ref.at[pl.ds(slot * n, n)]
 
     pairs = [(half(filter_hbm, 0), half(filt, 0)), (key_hbm, key), (value_hbm, value), (half(filter_hbm, 1), half(filt, 1)),
-             (gate_hbm, gate), (skip_hbm, skip_ref), (gain_hbm, gain_ref)]
+             (gate_hbm, gate), (weights_hbm, weights)]
     loads = [pltpu.make_async_copy(s, d, load_sems.at[i]) for i, (s, d) in enumerate(pairs)]
     table_loads = [pltpu.make_async_copy(s, d, table_sem.at[i]) for i, (s, d) in enumerate(zip(tables_hbm, tables_v))]
     for load in loads[:4]:
@@ -122,7 +122,8 @@
                 recv_sem=arrival, device_id={"ctx": p}, device_id_type=mesh_id,
             ).start()
 
-        def one(i, _):
+        def one(step, _):
+            i = n - step
             p = peer_of(i)
             if first:
                 later = functools.reduce(jnp.logical_and, [p != q for q in first])
@@ -170,7 +171,8 @@
     for load in loads[4:]:
         load.wait()
 
-    skip, gain = column(skip_ref[...]), column(gain_ref[...])
+    both = column(weights[...])
+    skip, gain = both[:channels], both[channels:]
     for c in range(0, channels, step):
         at = slice(c, c + step)
         gated[at] = gate[at].astype(F32)
@@ -289,11 +291,11 @@
         return pl.pallas_call(
             functools.partial(kernel, n, groups, channels * groups),
             out_shape=jax.ShapeDtypeStruct((channels, block), BF16),
-            in_specs=[hbm] * (6 + len(constants)),
-            out_specs=hbm,
+            in_specs=[hbm] * (5 + len(constants)),
+            out_specs=pl.BlockSpec(memory_space=pltpu.VMEM),
             scratch_shapes=[
                 half, half, half, full,
-                pltpu.VMEM((1, channels), F32), pltpu.VMEM((1, channels), F32),
+                pltpu.VMEM((1, 2 * channels), F32),
                 *[pltpu.VMEM(c.shape, c.dtype) for c in constants],
                 blocks, blocks, blocks, blocks, blocks, blocks,
                 pltpu.VMEM((rows, COLS), BF16), pltpu.VMEM((rows, COLS), BF16),
@@ -305,13 +307,13 @@
                 pltpu.VMEM((1, block), F32),
                 pltpu.VMEM((groups, 1, block), F32),
                 half,
-                DMA((7,)), DMA((len(constants),)), DMA((3,)), DMA((2, SLOTS)), DMA((SLOTS, n // min(8, n))),
+                DMA((6,)), DMA((len(constants),)), DMA((3,)), DMA((2, SLOTS)), DMA((SLOTS, n // min(8, n))),
                 DMA, DMA, DMA,
             ],
             compiler_params=pltpu.CompilerParams(
                 collective_id=0, has_side_effects=True, vmem_limit_bytes=VMEM_LIMIT),
             cost_estimate=pl.CostEstimate(flops=10**10, bytes_accessed=12 * 2**20, transcendentals=4096),
-        )(gate_in, key_in, value_in, long_filter, skip_weight.reshape(1, channels), norm_gain.reshape(1, channels),
+        )(gate_in, key_in, value_in, long_filter, jnp.concatenate([skip_weight, norm_gain]).reshape(1, 2 * channels),
           *[jnp.asarray(c) for c in constants])
 
     specs = (P("ch", "ctx"), P("ch", "ctx"), P("ch", "ctx"), P("ch", "ctx"), P("ch"), P("ch"))

time: 86.1 us -> 85.9 us (level)
  the two profiles are of different devices: /device:TPU:81 before, /device:TPU:65 now
where the time goes in v6:
time: 85.9 us; the launch traced here: 85.8 us
  Pallas kernels  84.3 us (98%)
    pallas_call x1, Pallas kernels, body(): pl.pallas_call(functools.partial(kernel, n, groups, channels * groups), o...  84.3 us

profile of v6, /device:TPU:65, one launch (start us, length us, event | category | flops | bytes accessed | tf_op | source)
XLA Modules:
  0.0 85.8 jit_solution(14844097185230391708)
XLA Ops:
  0.0 0.7 maximum_bitcast_fusion.weights_hbm
  0.7 84.3 %shard_map.82 = bf16[64,4096]{1,0:T(8,128)(2,1)S(1)} custom-call(bf16[64,4096]{1,0:T(8,128)(2,1)} %gate_hbm.1, bf16[64,4096]{1,0:T(8,128)(2,1)} %key_hbm.1, bf16[64,4096]{1,0:T(8,128)(2,1)} %value_hbm.1, f32[64,4096]{1,0:T(8,128)} %filter_hbm.1, f32[1,128]{1,0:T(1,128)S(1)} %maximum_bitcast_fusion.weights_hbm, bf16[2,3072,512]{2,1,0:T(8,128)(2,1)} %constant.4.clone.rest_0_, ...), custom_call_target="tpu_custom_call" | custom-call | flops 10000000000 | bytes 12582912 | tf_op jit(solution)/shard_map/pallas_call | solution.py:291
  85.0 0.8 copy.10
